TPU v7x, 128 devices: a whole 4x4x4 slice. The times are simulated.
128 devices in a mesh: row: 4 (over y), col: 4 (over x_lo, core), freq: 8 (over z, x_hi).
Axes of the slice: x: 4 (x_hi: 2, x_lo: 2; x = x_hi * 2 + x_lo), y: 4, z: 4, core: 2. Of those that a mesh axis runs over, the one named last changes fastest.
Arguments:
- traces: bfloat16 [1280, 224, 512], P(('row', 'col'), 'freq'), may hold values from -6 to 6
- window_mask: int32 [1280, 224], P(('row', 'col'), 'freq'), may hold values 0 or 1
Outputs:
- cross_spectra: bfloat16 [2, 256, 1280, 1280], P(None, 'freq', 'row', 'col')
All inputs are finite; a program needn't handle non-finite values. No bound on the sum of `window_mask` on one device may be relied on, other than what follows from the above.
Results may differ from a plain program's by a relative error of at most 0.0065.
Values may be sent and summed in bfloat16 or wider, within the bound.
A program may use at most 192 MiB of HBM per device.

v0:
```python
import math
import jax
import jax.numpy as jnp
from jax import lax
from jax.sharding import PartitionSpec as P

SAMPLES = 512
BINS = 256
epsilon = 1e-06


def dft_table():
    sample_idx = jnp.arange(SAMPLES, dtype=jnp.int32)
    bin_idx = jnp.arange(BINS, dtype=jnp.int32)
    phase = bin_idx[:, None] * sample_idx[None, :] % SAMPLES
    angles = 2.0 * math.pi / SAMPLES * phase.astype(jnp.float32)
    taper = 0.5 - 0.5 * jnp.cos(2.0 * math.pi / SAMPLES * sample_idx.astype(jnp.float32))
    stacked = jnp.stack(
        [taper[None, :] * jnp.cos(angles), -taper[None, :] * jnp.sin(angles)], axis=1
    )
    return stacked.reshape(2 * BINS, SAMPLES).astype(jnp.bfloat16)


def shards(traces, window_mask):
    dft = dft_table()
    spectrum = jnp.einsum("kt,swt->skw", dft, traces, preferred_element_type=jnp.float32)
    energy = jnp.mean(spectrum * spectrum, axis=1)
    factor = window_mask.astype(jnp.float32) * lax.rsqrt(energy + epsilon)
    whitened = (spectrum * factor[:, None, :]).astype(jnp.bfloat16)
    regrouped = lax.all_to_all(whitened, "freq", split_axis=1, concat_axis=2, tiled=True)
    everyone = lax.all_gather(regrouped, ("row", "col"), axis=0, tiled=True)
    block_rows = regrouped.shape[0] * lax.axis_size("col")
    row_stations = lax.dynamic_slice_in_dim(
        everyone, lax.axis_index("row") * block_rows, block_rows, 0
    )
    col_stations = lax.dynamic_slice_in_dim(
        everyone, lax.axis_index("col") * block_rows, block_rows, 0
    )
    windows_all = regrouped.shape[2]
    bins_here = regrouped.shape[1] // 2
    left_side = row_stations.reshape(row_stations.shape[0], bins_here, 2, windows_all)
    right_side = col_stations.reshape(col_stations.shape[0], bins_here, 2, windows_all)
    products = jnp.einsum(
        "ifcw,jfdw->fcdij", left_side, right_side, preferred_element_type=jnp.float32
    )
    norm_scale = 1.0 / math.sqrt(windows_all)
    real_part = (products[:, 0, 0] + products[:, 1, 1]) * norm_scale
    imag_part = (products[:, 1, 0] - products[:, 0, 1]) * norm_scale
    return jnp.stack([real_part, imag_part]).astype(jnp.bfloat16)


def solution(mesh):
    placed = (P(("row", "col"), "freq", None), P(("row", "col"), "freq"))
    return jax.shard_map(
        shards, mesh=mesh, in_specs=placed, out_specs=P(None, "freq", "row", "col"), check_vma=False
    )
```

profile of v0, /device:TPU:9, one launch (start us, length us, event | category | flops | bytes accessed | tf_op | source)
XLA Modules:
  0.0 428.0 jit_solution(7062251369111572887)
XLA Ops:
  6.5 0.0 copy-start
  6.5 0.0 copy-start.2
  6.5 0.0 all-gather.2.cloned.1.call-start
  6.6 2.2 multiply_convert_fusion.1
  8.9 0.1 pad_maximum_fusion.1
  8.9 0.5 copy.34
  9.5 0.2 reshape.179
  9.7 0.0 copy-done
  9.7 1.5 multiply_reduce_fusion
  11.2 0.0 copy-done.2
  11.2 0.4 fusion.7
  11.6 6.7 %copy.35 = bf16[80,512,28]{0,2,1:T(8,128)(2,1)} copy(bf16[80,512,28]{1,0,2:T(8,128)(2,1)S(1)} %fusion.7) | data formatting | bytes 4587520 | tf_op jit(solution)/shard_map/convert_element_type | solution.py:29
  18.3 57.5 %all_to_all.18 = bf16[80,512,28]{0,2,1:T(8,128)(2,1)S(1)} all-to-all(bf16[80,512,28]{0,2,1:T(8,128)(2,1)} %copy.35), channel_id=1, replica_groups=mesh['row'=4,'col'=4,'freq'=8] {'freq'}, dimensions={1} | all-to-all | bytes 4587520 | tf_op jit(solution)/shard_map/all_to_all | solution.py:30
  75.8 3.3 copy.37
  79.1 7.7 %copy.38 = bf16[80,64,224]{2,1,0:T(8,128)(2,1)} copy(bf16[80,64,224]{0,1,2:T(8,128)(2,1)} %bitcast.50) | data formatting | bytes 4587520 | tf_op jit(solution)/shard_map/all_to_all | solution.py:30
  86.7 0.0 all-gather.2.cloned.1.call-update
  86.7 209.4 %all-gather.2.cloned.1.call-done = bf16[1280,64,224]{2,1,0:T(8,128)(2,1)} async-done(((bf16[80,64,224]{2,1,0:T(8,128)(2,1)}), bf16[1280,64,224]{2,1,0:T(8,128)(2,1)}) %all-gather.2.cloned.1.call-update) | async-done | bytes 36700176 | tf_op jit(solution)/shard_map/all_gather | solution.py:31
  296.1 17.5 %constant_dynamic-slice_fusion = (bf16[320,64,224]{2,1,0:T(8,128)(2,1)}, bf16[320,64,224]{2,1,0:T(8,128)(2,1)}) fusion(bf16[1280,64,224]{2,1,0:T(8,128)(2,1)} %all-gather.2.cloned.1.call-done, s32[]{:T(128)S(6)} %select_n.28, s32[]{:T(128)S(6)} %select_n.27), kind=kLoop, calls=%fused_computation.30 | loop fusion | bytes 36700168 | tf_op jit(solution)/shard_map/dynamic_slice | solution.py:33
  313.7 13.9 %copy.40 = bf16[320,64,224]{2,0,1:T(8,128)(2,1)} copy(bf16[320,64,224]{2,1,0:T(8,128)(2,1)} %get-tuple-element.5) | data formatting | bytes 18350080 | tf_op jit(solution)/shard_map/dynamic_slice | solution.py:33
  327.6 14.2 %copy.39 = bf16[320,64,224]{2,0,1:T(8,128)(2,1)} copy(bf16[320,64,224]{2,1,0:T(8,128)(2,1)} %get-tuple-element.6) | data formatting | bytes 18350080 | tf_op jit(solution)/shard_map/dynamic_slice | solution.py:36
  341.8 29.1 %convolution_bitcast_fusion = f32[32,2,2,320,320]{3,4,1,2,0:T(8,128)} fusion(bf16[320,32,2,224,1]{3,0,4,2,1:T(8,128)(2,1)} %bitcast.48, bf16[320,32,2,224,1]{3,0,2,4,1:T(8,128)(2,1)} %bitcast.47), kind=kOutput, calls=%fused_computation | convolution fusion | flops 5872025600 | bytes 70778880 | tf_op jit(solution)/shard_map/ifcw,jfdw->fcdij/dot_general | solution.py:43
  370.9 10.9 %fusion.6 = bf16[1,32,320,320]{2,3,1,0:T(8,128)(2,1)S(1)} fusion(f32[32,2,2,320,320]{3,4,1,2,0:T(8,128)} %convolution_bitcast_fusion), kind=kLoop, calls=%fused_computation.11 | loop fusion | flops 9830400 | bytes 32768000 | tf_op jit(solution)/shard_map/mul | solution.py:48
  381.8 10.9 %fusion.5 = bf16[1,32,320,320]{2,3,1,0:T(8,128)(2,1)S(1)} fusion(f32[32,2,2,320,320]{3,4,1,2,0:T(8,128)} %convolution_bitcast_fusion), kind=kLoop, calls=%fused_computation.10 | loop fusion | flops 9830400 | bytes 32768000 | tf_op jit(solution)/shard_map/mul | solution.py:47
  392.7 0.0 copy-start.1
  392.7 7.5 %pad_maximum_fusion = bf16[2,32,320,320]{2,3,1,0:T(8,128)(2,1)} fusion(bf16[1,32,320,320]{2,3,1,0:T(8,128)(2,1)S(1)} %fusion.6, bf16[1,32,320,320]{2,3,1,0:T(8,128)(2,1)S(1)} %fusion.5), kind=kLoop, calls=%fused_computation.9 | loop fusion | flops 6553600 | bytes 26214400 | tf_op jit(solution)/shard_map/stack | solution.py:49
  400.2 20.9 %copy.44 = bf16[2,32,320,320]{3,2,1,0:T(8,128)(2,1)} copy(bf16[2,32,320,320]{2,3,1,0:T(8,128)(2,1)} %pad_maximum_fusion) | data formatting | bytes 26214400 | tf_op jit(solution)/shard_map/stack | solution.py:49
  421.1 0.0 copy-done.1
  (3 shorter events, 0.1 us)
Async XLA Ops:
  6.5 3.2 copy-start
  6.5 4.7 %copy-start.2 = (s32[80,28]{0,1:T(8,128)S(1)}, s32[80,28]{0,1:T(8,128)}, u32[]{:S(2)}) copy-start(s32[80,28]{0,1:T(8,128)} %param.3) | copy-start | bytes 26884
  6.5 289.6 %all-gather.2.cloned.1.call-start = ((), (), s32[]{:S(2)}) async-start(), calls=%async_computation.1 | async-start | bytes 44564480 | tf_op jit(solution)/shard_map/all_gather | solution.py:31
  392.7 28.4 %copy-start.1 = (bf16[80,28,512]{2,0,1:T(8,128)(2,1)S(1)}, bf16[80,28,512]{2,0,1:T(8,128)(2,1)}, u32[]{:S(2)}) copy-start(bf16[80,28,512]{2,0,1:T(8,128)(2,1)} %param.2) | copy-start | bytes 6881284
Sparse Core Ops, SparseCore 0:
  86.9 209.2 all-gather.1
where the time goes:
time: 429 us; the launch traced here: 428 us
  waiting for transfers between devices  209 us (49%)
  local copies, waits for them, and re-layouts  85 us (20%)
  blocking collectives  57.5 us (13%)
  other arithmetic  32.1 us (7%)
  matrix products  30.6 us (7%)
  between operations  13.5 us (3%)
    all_gather x1, waiting for transfers between devices, shards(): everyone = lax.all_gather(regrouped, ('row', 'col'), axis=0, tiled=True)  209 us
    all_to_all x1, blocking collectives, shards(): lax.all_to_all(whitened, 'freq', split_axis=1, concat_axis=2, tiled=True)  57.5 us
    dynamic_slice x2, local copies, waits for them, and re-layouts, shards(): lax.dynamic_slice_in_dim(everyone, lax.axis_index('row') * block_rows, bl...  31.4 us
    dot_general x1, matrix products, shards(): jnp.einsum('ifcw,jfdw->fcdij', left_side, right_side, preferred_element_t...  29.1 us
    another operation x1, local copies, waits for them, and re-layouts, shards(): return jnp.stack([real_part, imag_part]).astype(jnp.bfloat16)  20.9 us
    dynamic_slice x1, local copies, waits for them, and re-layouts, shards(): lax.dynamic_slice_in_dim(everyone, lax.axis_index('col') * block_rows, bl...  14.2 us
    mul x1, other arithmetic, shards(): real_part = (products[:, 0, 0] + products[:, 1, 1]) * norm_scale  10.9 us
    all_to_all x2, local copies, waits for them, and re-layouts, shards(): lax.all_to_all(whitened, 'freq', split_axis=1, concat_axis=2, tiled=True)  10.9 us
  transfers between devices with their start and end apart: 1, of which 1 were waited for; matrix products, arithmetic and copies ran while one was open for 0% of the time, Pallas kernels for 0%

commit v1 on v0

--- a/solution.py
+++ b/solution.py
@@ -27,7 +27,10 @@
     energy = jnp.mean(spectrum * spectrum, axis=1)
     factor = window_mask.astype(jnp.float32) * lax.rsqrt(energy + epsilon)
     whitened = (spectrum * factor[:, None, :]).astype(jnp.bfloat16)
-    regrouped = lax.all_to_all(whitened, "freq", split_axis=1, concat_axis=2, tiled=True)
+    regrouped = jnp.concatenate(
+        lax.all_to_all(jnp.stack(jnp.split(whitened, lax.axis_size("freq"), axis=1)), "freq", 0, 0),
+        axis=2,
+    )
     everyone = lax.all_gather(regrouped, ("row", "col"), axis=0, tiled=True)
     block_rows = regrouped.shape[0] * lax.axis_size("col")
     row_stations = lax.dynamic_slice_in_dim(

time: 429 us -> 397 us (0.925)
  local copies, waits for them, and re-layouts: 85 us -> 58.3 us
  blocking collectives: 57.5 us -> 52 us
    dynamic_slice x2 -> x1, local copies, waits for them, and re-layouts: 31.4 us -> 16.7 us  [shards(): lax.dynamic_slice_in_dim(everyone, lax.axis_index('row') * block_rows, bl...]
    dynamic_slice x1 -> x0, local copies, waits for them, and re-layouts: 14.2 us -> none  [shards(): lax.dynamic_slice_in_dim(everyone, lax.axis_index('col') * block_rows, bl...]
    all_to_all x2 -> x0, local copies, waits for them, and re-layouts: 10.9 us -> none  [shards(): lax.all_to_all(whitened, 'freq', split_axis=1, concat_axis=2, tiled=True)]
    another operation x0 -> x2, local copies, waits for them, and re-layouts: none -> 7.4 us  [shards(): jnp.stack(jnp.split(whitened, lax.axis_size('freq'), axis=1))]
    unnamed x6 -> x13, local copies, waits for them, and re-layouts: 0.01 us -> 6.75 us
    convert_element_type x1 -> x0, local copies, waits for them, and re-layouts: 6.7 us -> none  [shards(): whitened = (spectrum * factor[:, None, :]).astype(jnp.bfloat16)]
    reshape x0 -> x1, local copies, waits for them, and re-layouts: none -> 5.64 us  [shards(): jnp.concatenate(lax.all_to_all(jnp.stack(jnp.split(whitened, lax.axis_siz...]
    all_to_all x1, blocking collectives: 57.5 us -> 52 us  [shards(): lax.all_to_all(jnp.stack(jnp.split(whitened, lax.axis_size('freq'), axis=...]
where the time goes in v1:
time: 397 us; the launch traced here: 396 us
  waiting for transfers between devices  209 us (53%)
  local copies, waits for them, and re-layouts  58.3 us (15%)
  blocking collectives  52 us (13%)
  other arithmetic  32.1 us (8%)
  matrix products  30.6 us (8%)
  between operations  13.5 us (3%)
    all_gather x1, waiting for transfers between devices, shards(): everyone = lax.all_gather(regrouped, ('row', 'col'), axis=0, tiled=True)  209 us
    all_to_all x1, blocking collectives, shards(): lax.all_to_all(jnp.stack(jnp.split(whitened, lax.axis_size('freq'), axis=...  52 us
    dot_general x1, matrix products, shards(): jnp.einsum('ifcw,jfdw->fcdij', left_side, right_side, preferred_element_t...  29.1 us
    another operation x1, local copies, waits for them, and re-layouts, shards(): return jnp.stack([real_part, imag_part]).astype(jnp.bfloat16)  21.1 us
    dynamic_slice x1, local copies, waits for them, and re-layouts, shards(): lax.dynamic_slice_in_dim(everyone, lax.axis_index('row') * block_rows, bl...  16.7 us
    mul x1, other arithmetic, shards(): real_part = (products[:, 0, 0] + products[:, 1, 1]) * norm_scale  10.9 us
    mul x1, other arithmetic, shards(): imag_part = (products[:, 1, 0] - products[:, 0, 1]) * norm_scale  10.9 us
  transfers between devices with their start and end apart: 1, of which 1 were waited for; matrix products, arithmetic and copies ran while one was open for 0% of the time, Pallas kernels for 0%

profile of v1, /device:TPU:9, one launch (start us, length us, event | category | flops | bytes accessed | tf_op | source)
XLA Modules:
  0.0 395.7 jit_solution(9253051865816672454)
XLA Ops:
  6.5 0.0 copy-start
  6.5 0.0 all-gather.2.cloned.1.call-start
  6.6 2.2 multiply_convert_fusion.1
  8.9 0.1 pad_maximum_fusion.1
  8.9 0.5 copy.21
  9.5 0.2 reshape.187
  9.7 0.0 copy-done
  9.7 0.0 copy-start.2
  9.7 1.5 multiply_reduce_fusion
  11.2 0.0 copy-done.2
  11.2 0.4 fusion.7
  11.6 0.9 fusion.15
  12.5 1.0 fusion.14
  13.6 0.9 fusion.13
  14.5 1.0 fusion.12
  15.5 0.9 fusion.11
  16.4 1.0 fusion.10
  17.4 0.9 fusion.9
  18.4 1.0 fusion.8
  19.4 6.4 %copy.22 = bf16[8,80,64,28]{1,2,3,0:T(8,128)(2,1)} copy(bf16[8,80,64,28]{2,1,3,0:T(8,128)(2,1)} %fusion.8) | data formatting | bytes 4587520 | tf_op jit(solution)/shard_map/stack | solution.py:31
  25.8 52.0 %all_to_all.5 = bf16[8,80,64,28]{1,2,3,0:T(8,128)(2,1)} all-to-all(bf16[8,80,64,28]{1,2,3,0:T(8,128)(2,1)} %copy.22), channel_id=1, replica_groups=mesh['row'=4,'col'=4,'freq'=8] {'freq'}, dimensions={0} | all-to-all | bytes 4587520 | tf_op jit(solution)/shard_map/all_to_all | solution.py:31
  77.7 5.6 %copy.23 = bf16[80,64,224]{2,0,1:T(8,128)(2,1)} copy(bf16[80,64,224]{0,1,2:T(8,128)(2,1)} %bitcast.79) | data formatting | bytes 4587520 | tf_op jit(solution)/shard_map/reshape | solution.py:30
  83.4 0.0 all-gather.2.cloned.1.call-update
  83.4 209.3 %all-gather.2.cloned.1.call-done = bf16[1280,64,224]{2,0,1:T(8,128)(2,1)} async-done(((bf16[80,64,224]{2,0,1:T(8,128)(2,1)}), bf16[1280,64,224]{2,0,1:T(8,128)(2,1)}) %all-gather.2.cloned.1.call-update) | async-done | bytes 36700176 | tf_op jit(solution)/shard_map/all_gather | solution.py:34
  292.7 16.7 %constant_dynamic-slice_fusion = (bf16[320,64,224]{2,0,1:T(8,128)(2,1)}, bf16[320,64,224]{2,0,1:T(8,128)(2,1)}) fusion(bf16[1280,64,224]{2,0,1:T(8,128)(2,1)} %all-gather.2.cloned.1.call-done, s32[]{:T(128)S(6)} %select_n.28, s32[]{:T(128)S(6)} %select_n.27), kind=kLoop, calls=%fused_computation.46 | loop fusion | bytes 36700168 | tf_op jit(solution)/shard_map/dynamic_slice | solution.py:36
  309.4 29.1 %convolution_bitcast_fusion = f32[32,2,2,320,320]{3,4,1,2,0:T(8,128)} fusion(bf16[320,32,2,224,1]{3,0,4,2,1:T(8,128)(2,1)} %bitcast.78, bf16[320,32,2,224,1]{3,0,2,4,1:T(8,128)(2,1)} %bitcast.77), kind=kOutput, calls=%fused_computation | convolution fusion | flops 5872025600 | bytes 70778880 | tf_op jit(solution)/shard_map/ifcw,jfdw->fcdij/dot_general | solution.py:46
  338.5 10.9 %fusion.6 = bf16[1,32,320,320]{2,3,1,0:T(8,128)(2,1)S(1)} fusion(f32[32,2,2,320,320]{3,4,1,2,0:T(8,128)} %convolution_bitcast_fusion), kind=kLoop, calls=%fused_computation.11 | loop fusion | flops 9830400 | bytes 32768000 | tf_op jit(solution)/shard_map/mul | solution.py:51
  349.4 10.9 %fusion.5 = bf16[1,32,320,320]{2,3,1,0:T(8,128)(2,1)S(1)} fusion(f32[32,2,2,320,320]{3,4,1,2,0:T(8,128)} %convolution_bitcast_fusion), kind=kLoop, calls=%fused_computation.10 | loop fusion | flops 9830400 | bytes 32768000 | tf_op jit(solution)/shard_map/mul | solution.py:50
  360.3 7.5 %pad_maximum_fusion = bf16[2,32,320,320]{2,3,1,0:T(8,128)(2,1)} fusion(bf16[1,32,320,320]{2,3,1,0:T(8,128)(2,1)S(1)} %fusion.6, bf16[1,32,320,320]{2,3,1,0:T(8,128)(2,1)S(1)} %fusion.5), kind=kLoop, calls=%fused_computation.9 | loop fusion | flops 6553600 | bytes 26214400 | tf_op jit(solution)/shard_map/stack | solution.py:52
  367.8 0.0 copy-start.1
  367.8 21.1 %copy.27 = bf16[2,32,320,320]{3,2,1,0:T(8,128)(2,1)} copy(bf16[2,32,320,320]{2,3,1,0:T(8,128)(2,1)} %pad_maximum_fusion) | data formatting | bytes 26214400 | tf_op jit(solution)/shard_map/stack | solution.py:52
  388.8 0.0 copy-done.1
  (3 shorter events, 0.1 us)
Async XLA Ops:
  6.5 3.2 copy-start
  6.5 286.2 %all-gather.2.cloned.1.call-start = ((), (), s32[]{:S(2)}) async-start(), calls=%async_computation.1 | async-start | bytes 44564480 | tf_op jit(solution)/shard_map/all_gather | solution.py:34
  9.7 1.5 copy-start.2
  367.8 21.1 %copy-start.1 = (bf16[80,28,512]{2,0,1:T(8,128)(2,1)S(1)}, bf16[80,28,512]{2,0,1:T(8,128)(2,1)}, u32[]{:S(2)}) copy-start(bf16[80,28,512]{2,0,1:T(8,128)(2,1)} %param.2) | copy-start | bytes 6881284
Sparse Core Ops, SparseCore 0:
  83.5 209.1 all-gather.1

commit v2 on v0

--- a/solution.py
+++ b/solution.py
@@ -28,7 +28,12 @@
     factor = window_mask.astype(jnp.float32) * lax.rsqrt(energy + epsilon)
     whitened = (spectrum * factor[:, None, :]).astype(jnp.bfloat16)
     regrouped = lax.all_to_all(whitened, "freq", split_axis=1, concat_axis=2, tiled=True)
-    everyone = lax.all_gather(regrouped, ("row", "col"), axis=0, tiled=True)
+    everyone = jnp.concatenate(
+        lax.all_to_all(
+            jnp.stack([regrouped] * lax.axis_size(("row", "col"))), ("row", "col"), 0, 0
+        ),
+        axis=0,
+    )
     block_rows = regrouped.shape[0] * lax.axis_size("col")
     row_stations = lax.dynamic_slice_in_dim(
         everyone, lax.axis_index("row") * block_rows, block_rows, 0

time: 429 us -> 710 us (1.66)
  waiting for transfers between devices: 209 us -> 453 us
  local copies, waits for them, and re-layouts: 85 us -> 126 us
  between operations: 13.5 us -> 0.1 us
  starting transfers between devices: 0.01 us -> 7.99 us
    all_to_all x0 -> x1, waiting for transfers between devices: none -> 453 us  [shards(): lax.all_to_all(jnp.stack([regrouped] * lax.axis_size(('row', 'col'))), ('...]
    all_gather x1 -> x0, waiting for transfers between devices: 209 us -> none  [shards(): everyone = lax.all_gather(regrouped, ('row', 'col'), axis=0, tiled=True)]
    all_to_all x0 -> x1, local copies, waits for them, and re-layouts: none -> 28.5 us  [shards(): lax.all_to_all(jnp.stack([regrouped] * lax.axis_size(('row', 'col'))), ('...]
    another operation x0 -> x2, local copies, waits for them, and re-layouts: none -> 20.6 us  [shards(): jnp.stack([regrouped] * lax.axis_size(('row', 'col')))]
    all_to_all x0 -> x1, starting transfers between devices: none -> 7.99 us  [shards(): lax.all_to_all(jnp.stack([regrouped] * lax.axis_size(('row', 'col'))), ('...]
    all_to_all x2 -> x1, local copies, waits for them, and re-layouts: 10.9 us -> 3.26 us  [shards(): lax.all_to_all(whitened, 'freq', split_axis=1, concat_axis=2, tiled=True)]
where the time goes in v2:
time: 710 us; the launch traced here: 707 us
  waiting for transfers between devices  453 us (64%)
  local copies, waits for them, and re-layouts  126 us (18%)
  blocking collectives  57.5 us (8%)
  other arithmetic  32.1 us (5%)
  matrix products  30.6 us (4%)
  starting transfers between devices  7.99 us (1%)
    all_to_all x1, waiting for transfers between devices, shards(): lax.all_to_all(jnp.stack([regrouped] * lax.axis_size(('row', 'col'))), ('...  453 us
    all_to_all x1, blocking collectives, shards(): lax.all_to_all(whitened, 'freq', split_axis=1, concat_axis=2, tiled=True)  57.5 us
    dynamic_slice x2, local copies, waits for them, and re-layouts, shards(): lax.dynamic_slice_in_dim(everyone, lax.axis_index('row') * block_rows, bl...  31.6 us
    dot_general x1, matrix products, shards(): jnp.einsum('ifcw,jfdw->fcdij', left_side, right_side, preferred_element_t...  29.1 us
    all_to_all x1, local copies, waits for them, and re-layouts, shards(): lax.all_to_all(jnp.stack([regrouped] * lax.axis_size(('row', 'col'))), ('...  28.5 us
    another operation x1, local copies, waits for them, and re-layouts, shards(): return jnp.stack([real_part, imag_part]).astype(jnp.bfloat16)  20.9 us
    another operation x2, local copies, waits for them, and re-layouts, shards(): jnp.stack([regrouped] * lax.axis_size(('row', 'col')))  20.6 us
  transfers between devices with their start and end apart: 1, of which 1 were waited for; matrix products, arithmetic and copies ran while one was open for 0% of the time, Pallas kernels for 0%

profile of v2, /device:TPU:9, one launch (start us, length us, event | category | flops | bytes accessed | tf_op | source)
XLA Modules:
  0.0 707.3 jit_solution(5081409580307430344)
XLA Ops:
  0.0 0.0 copy-start
  0.0 0.0 copy-start.2
  0.1 2.2 multiply_convert_fusion.1
  2.4 0.1 pad_maximum_fusion.1
  2.4 0.5 copy.43
  3.0 0.2 reshape.186
  3.2 0.0 copy-done
  3.2 1.5 multiply_reduce_fusion
  4.7 0.0 copy-done.2
  4.7 0.4 fusion.7
  5.1 6.7 copy.44
  11.8 57.5 %all_to_all.20 = bf16[80,512,28]{0,2,1:T(8,128)(2,1)S(1)} all-to-all(bf16[80,512,28]{0,2,1:T(8,128)(2,1)} %copy.44), channel_id=1, replica_groups=mesh['row'=4,'col'=4,'freq'=8] {'freq'}, dimensions={1} | all-to-all | bytes 4587520 | tf_op jit(solution)/shard_map/all_to_all | solution.py:30
  69.3 3.3 copy.46
  72.5 5.6 copy.47
  78.2 15.0 %stack.12 = bf16[16,80,64,224]{3,1,2,0:T(8,128)(2,1)} broadcast(bf16[80,64,224]{2,0,1:T(8,128)(2,1)} %copy.47), dimensions={1,2,3} | broadcast | bytes 38993920 | tf_op jit(solution)/shard_map/stack | solution.py:33
  93.1 8.0 %all-to-all-start.1 = ((bf16[16,80,64,224]{3,1,2,0:T(8,128)(2,1)}), bf16[16,80,64,224]{3,1,2,0:T(8,128)(2,1)}, u32[]{:S(2)}, u32[]{:S(2)}) async-start(bf16[16,80,64,224]{3,1,2,0:T(8,128)(2,1)} %stack.12), calls=%async_computation.1 | async-start | bytes 83886080 | tf_op jit(solution)/shard_map/all_to_all | solution.py:32
  101.1 452.8 %all-to-all-done.1 = bf16[16,80,64,224]{3,1,2,0:T(8,128)(2,1)} async-done(((bf16[16,80,64,224]{3,1,2,0:T(8,128)(2,1)}), bf16[16,80,64,224]{3,1,2,0:T(8,128)(2,1)}, u32[]{:S(2)}, u32[]{:S(2)}) %all-to-all-start.1) | async-done | bytes 36700192 | tf_op jit(solution)/shard_map/all_to_all | solution.py:32
  554.0 28.5 %copy.48 = bf16[16,80,64,224]{3,2,1,0:T(8,128)(2,1)} copy(bf16[16,80,64,224]{3,1,2,0:T(8,128)(2,1)} %all-to-all-done.1) | data formatting | bytes 73400320 | tf_op jit(solution)/shard_map/all_to_all | solution.py:32
  582.5 17.5 %constant_dynamic-slice_fusion = (bf16[320,64,224]{2,1,0:T(8,128)(2,1)}, bf16[320,64,224]{2,1,0:T(8,128)(2,1)}) fusion(bf16[1280,64,224]{2,1,0:T(8,128)(2,1)} %bitcast.48, s32[]{:T(128)S(6)} %select_n.28, s32[]{:T(128)S(6)} %select_n.27), kind=kLoop, calls=%fused_computation.30 | loop fusion | bytes 36700168 | tf_op jit(solution)/shard_map/dynamic_slice | solution.py:38
  600.0 13.9 %copy.49 = bf16[320,64,224]{2,0,1:T(8,128)(2,1)} copy(bf16[320,64,224]{2,1,0:T(8,128)(2,1)} %get-tuple-element.6) | data formatting | bytes 18350080 | tf_op jit(solution)/shard_map/dynamic_slice | solution.py:41
  613.9 14.1 %copy.50 = bf16[320,64,224]{2,0,1:T(8,128)(2,1)} copy(bf16[320,64,224]{2,1,0:T(8,128)(2,1)} %get-tuple-element.5) | data formatting | bytes 18350080 | tf_op jit(solution)/shard_map/dynamic_slice | solution.py:38
  628.0 29.1 %convolution_bitcast_fusion = f32[32,2,2,320,320]{3,4,1,2,0:T(8,128)} fusion(bf16[320,32,2,224,1]{3,0,4,2,1:T(8,128)(2,1)} %bitcast.49, bf16[320,32,2,224,1]{3,0,2,4,1:T(8,128)(2,1)} %bitcast.50), kind=kOutput, calls=%fused_computation | convolution fusion | flops 5872025600 | bytes 70778880 | tf_op jit(solution)/shard_map/ifcw,jfdw->fcdij/dot_general | solution.py:48
  657.0 10.9 %fusion.6 = bf16[1,32,320,320]{2,3,1,0:T(8,128)(2,1)S(1)} fusion(f32[32,2,2,320,320]{3,4,1,2,0:T(8,128)} %convolution_bitcast_fusion), kind=kLoop, calls=%fused_computation.11 | loop fusion | flops 9830400 | bytes 32768000 | tf_op jit(solution)/shard_map/mul | solution.py:53
  667.9 10.9 %fusion.5 = bf16[1,32,320,320]{2,3,1,0:T(8,128)(2,1)S(1)} fusion(f32[32,2,2,320,320]{3,4,1,2,0:T(8,128)} %convolution_bitcast_fusion), kind=kLoop, calls=%fused_computation.10 | loop fusion | flops 9830400 | bytes 32768000 | tf_op jit(solution)/shard_map/mul | solution.py:52
  678.9 0.0 copy-start.1
  678.9 7.5 %pad_maximum_fusion = bf16[2,32,320,320]{2,3,1,0:T(8,128)(2,1)} fusion(bf16[1,32,320,320]{2,3,1,0:T(8,128)(2,1)S(1)} %fusion.6, bf16[1,32,320,320]{2,3,1,0:T(8,128)(2,1)S(1)} %fusion.5), kind=kLoop, calls=%fused_computation.9 | loop fusion | flops 6553600 | bytes 26214400 | tf_op jit(solution)/shard_map/stack | solution.py:54
  686.4 20.9 %copy.54 = bf16[2,32,320,320]{3,2,1,0:T(8,128)(2,1)} copy(bf16[2,32,320,320]{2,3,1,0:T(8,128)(2,1)} %pad_maximum_fusion) | data formatting | bytes 26214400 | tf_op jit(solution)/shard_map/stack | solution.py:54
  707.3 0.0 copy-done.1
  (3 shorter events, 0.1 us)
Async XLA Ops:
  0.0 3.2 copy-start
  0.0 4.7 copy-start.2
  93.1 460.8 %all-to-all-start.1 = ((bf16[16,80,64,224]{3,1,2,0:T(8,128)(2,1)}), bf16[16,80,64,224]{3,1,2,0:T(8,128)(2,1)}, u32[]{:S(2)}, u32[]{:S(2)}) async-start(bf16[16,80,64,224]{3,1,2,0:T(8,128)(2,1)} %stack.12), calls=%async_computation.1 | async-start | bytes 83886080 | tf_op jit(solution)/shard_map/all_to_all | solution.py:32
  678.9 28.4 %copy-start.1 = (bf16[80,28,512]{2,0,1:T(8,128)(2,1)S(1)}, bf16[80,28,512]{2,0,1:T(8,128)(2,1)}, u32[]{:S(2)}) copy-start(bf16[80,28,512]{2,0,1:T(8,128)(2,1)} %param.2) | copy-start | bytes 6881284
